TPU v7x, 32 devices: a whole 2x2x4 slice. The times are simulated.
32 devices in a mesh: row: 8 (over y, x, core), col: 4 (over z).
Axes of the slice: x: 2, y: 2, z: 4, core: 2. Of those that a mesh axis runs over, the one named last changes fastest.
Arguments:
- radar_tiles: bfloat16 [512, 256, 256], P('row', 'col'), may hold values from -6 to 6
- conv_scale: float32 [256], replicated, may hold values from 0.5 to 1.5
- conv_shift: float32 [256], replicated, may hold values from -3 to 3
- expand_weight: bfloat16 [256, 1024], replicated, may hold values from -0.375 to 0.375
- expand_bias: float32 [1024], replicated, may hold values from -3 to 3
- depth_kernel: float32 [3, 3, 1024], replicated, may hold values from -2 to 2
- depth_bias: float32 [1024], replicated, may hold values from -3 to 3
- project_weight: bfloat16 [1024, 256], replicated, may hold values from -0.1875 to 0.1875
- block_gains: float32 [2, 256], replicated, may hold values from 0.5 to 1.5
- block_entry: bfloat16 [256, 768], replicated, may hold values from -0.375 to 0.375
- block_leave: bfloat16 [256, 256], replicated, may hold values from -0.375 to 0.375
- block_offsets: float32 [8, 64, 64], replicated, may hold values from -6 to 6
- block_widen: bfloat16 [256, 1024], replicated, may hold values from -0.375 to 0.375
- block_shrink: bfloat16 [1024, 256], replicated, may hold values from -0.1875 to 0.1875
- grid_gains: float32 [2, 256], replicated, may hold values from 0.5 to 1.5
- grid_entry: bfloat16 [256, 768], replicated, may hold values from -0.375 to 0.375
- grid_leave: bfloat16 [256, 256], replicated, may hold values from -0.375 to 0.375
- grid_offsets: float32 [8, 64, 64], replicated, may hold values from -6 to 6
- grid_widen: bfloat16 [256, 1024], replicated, may hold values from -0.375 to 0.375
- grid_shrink: bfloat16 [1024, 256], replicated, may hold values from -0.1875 to 0.1875
Outputs:
- refined: bfloat16 [512, 256, 256], P('row', 'col')
All inputs are finite; a program needn't handle non-finite values.
Results may differ from a plain program's by a relative error of at most 0.015.
Values may be sent and summed in bfloat16 or wider, within the bound.
A program may use at most 128 MiB of HBM per device.

v0:
```python
import math

import jax
import jax.numpy as jnp
from jax import lax
from jax.sharding import PartitionSpec as P

WIN = 8


epsilon = 1e-05


def with_halo(block, sides, width):
    for axis, dim in sides:
        count = lax.axis_size(axis)
        forward = [(i, i + 1) for i in range(count - 1)]
        backward = [(target, source) for source, target in forward]
        low = lax.ppermute(
            lax.slice_in_dim(block, block.shape[dim] - width, None, axis=dim), axis, forward
        )
        high = lax.ppermute(lax.slice_in_dim(block, 0, width, axis=dim), axis, backward)
        block = jnp.concatenate([low, block, high], axis=dim)
    return block


def layer_norm(values, gain_row):
    center = values - jnp.mean(values, axis=-1, keepdims=True)
    spread = jnp.mean(center * center, axis=-1, keepdims=True)
    return center * lax.rsqrt(spread + epsilon) * gain_row


def attend(
    windows, norm_gains, entry_weight, leave_weight, offset_table, widen_weight, shrink_weight
):
    win_count, positions, channels = windows.shape
    head_count = offset_table.shape[0]
    head_size = channels // head_count
    flattened = windows.reshape(-1, channels)
    lifted = layer_norm(flattened.astype(jnp.float32), norm_gains[0]).astype(jnp.bfloat16)
    projected = jnp.dot(lifted, entry_weight, preferred_element_type=jnp.float32).astype(
        jnp.bfloat16
    )
    projected = projected.reshape(win_count, positions, 3, head_count, head_size)
    query_rows = projected[:, :, 0]
    key_rows = projected[:, :, 1]
    value_rows = projected[:, :, 2]
    score_scale = 1.0 / math.sqrt(head_size)
    scores = (
        jnp.einsum("nqhd,nkhd->nhqk", query_rows, key_rows, preferred_element_type=jnp.float32)
        * score_scale
        + offset_table
    )
    weights = jnp.exp(scores)
    weights = (weights / jnp.sum(weights, axis=-1, keepdims=True)).astype(jnp.bfloat16)
    mixture = jnp.einsum("nhqk,nkhd->nqhd", weights, value_rows, preferred_element_type=jnp.float32)
    mixture = mixture.astype(jnp.bfloat16).reshape(-1, channels)
    attended = (
        flattened.astype(jnp.float32)
        + jnp.dot(mixture, leave_weight, preferred_element_type=jnp.float32)
    ).astype(jnp.bfloat16)
    second = layer_norm(attended.astype(jnp.float32), norm_gains[1]).astype(jnp.bfloat16)
    hidden = jax.nn.gelu(jnp.dot(second, widen_weight, preferred_element_type=jnp.float32)).astype(
        jnp.bfloat16
    )
    result = attended.astype(jnp.float32) + jnp.dot(
        hidden, shrink_weight, preferred_element_type=jnp.float32
    )
    return result.astype(jnp.bfloat16).reshape(win_count, positions, channels)


def expand_cells(cells, expand_weight, expand_bias):
    first_dim, second_dim, channels = cells.shape
    product = jnp.dot(
        cells.reshape(-1, channels), expand_weight, preferred_element_type=jnp.float32
    )
    return (
        jax.nn.gelu(product + expand_bias).astype(jnp.bfloat16).reshape(first_dim, second_dim, -1)
    )


def shards(
    radar_tiles,
    conv_scale,
    conv_shift,
    expand_weight,
    expand_bias,
    depth_kernel,
    depth_bias,
    project_weight,
    block_gains,
    block_entry,
    block_leave,
    block_offsets,
    block_widen,
    block_shrink,
    grid_gains,
    grid_entry,
    grid_leave,
    grid_offsets,
    grid_widen,
    grid_shrink,
):
    rows_here, cols_here, channels = radar_tiles.shape
    inner_width = expand_weight.shape[1]
    source = radar_tiles.astype(jnp.float32)
    normed = (source * conv_scale + conv_shift).astype(jnp.bfloat16)
    inner_cells = expand_cells(normed, expand_weight, expand_bias)
    padded = with_halo(inner_cells, (("row", 0), ("col", 1)), 1)
    summed = jnp.zeros((rows_here, cols_here, inner_width), jnp.float32)
    for shift_row in range(3):
        for shift_col in range(3):
            summed = (
                summed
                + padded[
                    shift_row : shift_row + rows_here, shift_col : shift_col + cols_here
                ].astype(jnp.float32)
                * depth_kernel[shift_row, shift_col]
            )
    activated = jax.nn.gelu(summed + depth_bias).astype(jnp.bfloat16)
    product = jnp.dot(
        activated.reshape(-1, inner_width), project_weight, preferred_element_type=jnp.float32
    )
    section_one = (source + product.reshape(rows_here, cols_here, channels)).astype(jnp.bfloat16)
    blocks = section_one.reshape(rows_here // WIN, WIN, cols_here // WIN, WIN, channels).transpose(
        0, 2, 1, 3, 4
    )
    blocks = blocks.reshape(-1, WIN * WIN, channels)
    attended_tiles = attend(
        blocks, block_gains, block_entry, block_leave, block_offsets, block_widen, block_shrink
    )
    section_two = attended_tiles.reshape(
        rows_here // WIN, cols_here // WIN, WIN, WIN, channels
    ).transpose(0, 2, 1, 3, 4)
    section_two = section_two.reshape(rows_here, cols_here, channels)
    row_count = lax.axis_size("row")
    col_count = lax.axis_size("col")
    held_rows = max(1, WIN // row_count)
    held_cols = max(1, WIN // col_count)
    row_phases = max(1, row_count // WIN)
    col_phases = max(1, col_count // WIN)
    row_cells = rows_here // held_rows
    col_cells = cols_here // held_cols
    devices = row_count * col_count
    per_piece = row_cells * col_cells // devices
    outgoing = section_two.reshape(held_rows, row_cells, held_cols, col_cells, channels).transpose(
        1, 3, 0, 2, 4
    )
    outgoing = outgoing.reshape(devices, per_piece, held_rows, held_cols, channels)
    arrived = lax.all_to_all(outgoing, ("row", "col"), split_axis=0, concat_axis=0, tiled=True)
    slot_count = arrived.shape[1]
    regroup_slot_count = arrived.shape[1]
    grouped = arrived.reshape(
        row_count // row_phases,
        row_phases,
        col_count // col_phases,
        col_phases,
        regroup_slot_count,
        held_rows,
        held_cols,
        channels,
    )
    grouped = grouped.transpose(1, 3, 4, 0, 5, 2, 6, 7).reshape(-1, WIN * WIN, channels)
    finished = attend(
        grouped, grid_gains, grid_entry, grid_leave, grid_offsets, grid_widen, grid_shrink
    )
    finished = finished.reshape(
        row_phases,
        col_phases,
        regroup_slot_count,
        row_count // row_phases,
        held_rows,
        col_count // col_phases,
        held_cols,
        channels,
    )
    returning = finished.transpose(3, 0, 5, 1, 2, 4, 6, 7).reshape(
        devices, slot_count, held_rows, held_cols, channels
    )
    returned = lax.all_to_all(returning, ("row", "col"), split_axis=0, concat_axis=0, tiled=True)
    finished_tiles = returned.reshape(
        row_cells, col_cells, held_rows, held_cols, channels
    ).transpose(2, 0, 3, 1, 4)
    return finished_tiles.reshape(rows_here, cols_here, channels)


def solution(mesh):
    return jax.shard_map(
        shards,
        mesh=mesh,
        in_specs=(
            P("row", "col", None),
            P(),
            P(),
            P(),
            P(),
            P(),
            P(),
            P(),
            P(),
            P(),
            P(),
            P(),
            P(),
            P(),
            P(),
            P(),
            P(),
            P(),
            P(),
            P(),
        ),
        out_specs=P("row", "col", None),
        check_vma=False,
    )
```

profile of v0, /device:TPU:1, one launch (start us, length us, event | category | flops | bytes accessed | tf_op | source)
XLA Modules:
  0.0 454.2 jit_solution(1873179815434759581)
XLA Ops:
  2.3 7.1 %fusion.7 = bf16[4096,1024]{1,0:T(8,128)(2,1)S(1)} fusion(bf16[4096,256]{1,0:T(8,128)(2,1)S(1)} %bitcast.141, bf16[256,1024]{1,0:T(8,128)(2,1)S(1)} %copy-done, f32[1024]{0:T(1024)} %param.24), kind=kOutput, calls=%fused_computation.11 | convolution fusion | flops 2189426688 | bytes 11014144 | tf_op jit(solution)/shard_map/dot_general | solution.py:74
  36.5 13.8 %maximum_maximum_fusion = (bf16[66,65,1024]{2,1,0:T(8,128)(2,1)}, bf16[66,65,1024]{2,1,0:T(8,128)(2,1)}) fusion(bf16[1,64,1024]{2,1,0:T(8,128)(2,1)S(1)} %collective-permute-done.1, bf16[64,64,1024]{2,1,0:T(8,128)(2,1)S(1)} %bitcast.127, bf16[1,64,1024]{2,1,0:T(8,128)(2,1)S(1)} %collective-permute-done, bf16[66,1,1024]{2,1,0:T(2,128)(2,1)S(1)} %collective-permute-done.2, ...), kind=kLoop, calls=%fused_computation.42 | loop fusion | flops 70287360 | bytes 26492928 | tf_op jit(solution)/shard_map/concatenate | solution.py:23
  50.3 32.6 %fusion.70 = bf16[64,64,256]{2,1,0:T(8,128)(2,1)} fusion(bf16[64,64,256]{2,1,0:T(8,128)(2,1)} %param.20, bf16[64,64,1024]{2,1,0:T(8,128)(2,1)S(1)} %bitcast.128, bf16[66,65,1024]{2,1,0:T(8,128)(2,1)} %get-tuple-element.12, bf16[1,64,1024]{2,1,0:T(8,128)(2,1)S(1)} %collective-permute-done.1, bf16[66,65,1024]{2,1,0:T(8,128)(2,1)} %get-tuple-element.11, ...), kind=kOutput, calls=%fused_computation.81 | convolution fusion | flops 2310012928 | bytes 63741952 | tf_op jit(solution)/shard_map/dot_general | solution.py:121
  103.4 8.7 %copy.76 = bf16[4096,768]{0,1:T(8,128)(2,1)} copy(bf16[4096,768]{1,0:T(8,128)(2,1)} %convolution_convert_fusion.1) | data formatting | bytes 12582912 | tf_op jit(solution)/shard_map/convert_element_type | solution.py:41
  112.1 17.9 %reshape.154 = bf16[64,64,3,8,32]{1,0,4,3,2:T(8,128)(2,1)} reshape(bf16[4096,768]{0,1:T(8,128)(2,1)} %copy.76) | data formatting | bytes 12582912 | tf_op jit(solution)/shard_map/reshape | solution.py:44
  129.9 8.5 %fusion.116 = (bf16[64,64,1,8,32]{1,0,4,3,2:T(8,128)(2,1)}, bf16[64,64,1,8,32]{1,0,4,3,2:T(8,128)(2,1)S(1)}, bf16[64,64,1,8,32]{1,0,4,3,2:T(8,128)(2,1)}) fusion(bf16[64,64,3,8,32]{1,0,4,3,2:T(8,128)(2,1)} %reshape.154), kind=kLoop, calls=%fused_computation.142 | loop fusion | bytes 12582912 | tf_op jit(solution)/shard_map/slice | solution.py:47
  138.4 20.3 %fusion.32 = (f32[64,8,64]{2,1,0:T(8,128)S(1)}, f32[64,8,64,64]{2,3,1,0:T(8,128)}) fusion(f32[8,64,64]{1,2,0:T(8,128)S(1)} %copy.80, bf16[64,64,1,8,32]{1,0,4,3,2:T(8,128)(2,1)} %get-tuple-element.10, bf16[64,64,1,8,32]{1,0,4,3,2:T(8,128)(2,1)S(1)} %get-tuple-element.9), kind=kOutput, calls=%fused_computation.40 | convolution fusion | flops 140476416 | bytes 12845056 | tf_op jit(solution)/shard_map/nqhd,nkhd->nhqk/dot_general | solution.py:50
  158.8 19.5 %convert_bitcast_fusion.2 = bf16[64,64,8,32]{1,3,2,0:T(8,128)(2,1)} fusion(f32[64,8,64,64]{2,3,1,0:T(8,128)} %get-tuple-element.31, f32[64,8,64]{2,1,0:T(8,128)S(1)} %get-tuple-element.30, f32[8,64,64]{1,2,0:T(8,128)S(1)} %copy.80, bf16[64,64,1,8,32]{1,0,4,3,2:T(8,128)(2,1)} %get-tuple-element.8), kind=kOutput, calls=%fused_computation.99 | convolution fusion | flops 143654912 | bytes 12845056 | tf_op jit(solution)/shard_map/nhqk,nkhd->nqhd/dot_general | solution.py:56
  178.2 7.1 %copy.82 = bf16[64,64,8,32]{1,0,3,2:T(8,128)(2,1)} copy(bf16[64,64,8,32]{1,3,2,0:T(8,128)(2,1)} %convert_bitcast_fusion.2) | data formatting | bytes 4194304 | tf_op jit(solution)/shard_map/convert_element_type | solution.py:57
  185.3 5.7 %reshape.155 = bf16[4096,256]{0,1:T(8,128)(2,1)S(1)} reshape(bf16[64,64,8,32]{1,0,3,2:T(8,128)(2,1)} %copy.82) | data formatting | bytes 4194304 | tf_op jit(solution)/shard_map/reshape | solution.py:57
  197.2 9.0 %fusion.48 = bf16[4096,256]{1,0:T(8,128)(2,1)S(1)} fusion(bf16[1024,256]{1,0:T(8,128)(2,1)S(1)} %copy-done.17, bf16[4096,256]{1,0:T(8,128)(2,1)} %copy-done.5, bf16[256,1024]{1,0:T(8,128)(2,1)} %param.32, f32[256]{0:T(256)S(1)} %bitcast.153, f32[4096]{0:T(1024)S(1)} %add_rsqrt_fusion.3, f32[4096]{0:T(1024)S(1)} %broadcast_multiply_fusion.3), kind=kOutput, calls=%fused_computation.65 | convolution fusion | flops 4341104640 | bytes 5276672 | tf_op jit(solution)/shard_map/dot_general | solution.py:66
  208.2 6.9 %all-to-all-start = ((bf16[32,64,1,2,256]{4,1,3,2,0:T(8,128)(2,1)}), bf16[32,64,1,2,256]{4,1,3,2,0:T(8,128)(2,1)S(1)}, u32[]{:S(2)}, u32[]{:S(2)}) async-start(bf16[32,64,1,2,256]{4,1,3,2,0:T(8,128)(2,1)} %copy.85), calls=%async_computation | async-start | bytes 4194304 | tf_op jit(solution)/shard_map/all_to_all | solution.py:150
  215.3 48.0 %all-to-all-done = bf16[32,64,1,2,256]{4,1,3,2,0:T(8,128)(2,1)S(1)} async-done(((bf16[32,64,1,2,256]{4,1,3,2,0:T(8,128)(2,1)}), bf16[32,64,1,2,256]{4,1,3,2,0:T(8,128)(2,1)S(1)}, u32[]{:S(2)}, u32[]{:S(2)}) %all-to-all-start) | async-done | bytes 2097184 | tf_op jit(solution)/shard_map/all_to_all | solution.py:150
  272.4 6.2 %multiply_reduce_fusion = f32[64,8,4,2]{3,2,1,0:T(4,128)S(1)} fusion(f32[64,8,4,2]{3,2,1,0:T(4,128)S(1)} %broadcast_multiply_fusion, f32[8,1,4,1,64,1,2,256]{7,4,6,2,0,5,3,1:T(8,128)S(1)} %convert.11), kind=kLoop, calls=%fused_computation.98 | loop fusion | flops 3141632 | bytes 4227072 | tf_op jit(solution)/shard_map/reduce_sum | solution.py:29
  280.8 6.1 %reshape.163 = f32[4096,256]{1,0:T(8,128)} reshape(f32[1,1,64,8,1,4,2,256]{7,6,5,3,2,4,1,0:T(2,128)} %bitcast.134) | data formatting | bytes 8388608 | tf_op jit(solution)/shard_map/convert_element_type | solution.py:59
  286.9 6.3 %convolution_convert_fusion = bf16[4096,768]{1,0:T(8,128)(2,1)} fusion(bf16[256,768]{1,0:T(8,128)(2,1)S(1)} %copy-done.8, f32[4096,256]{1,0:T(8,128)} %reshape.163, f32[256]{0:T(256)S(1)} %bitcast.142, f32[4096]{0:T(1024)S(1)} %rsqrt.42, f32[4096]{0:T(1024)S(1)} %div.52), kind=kOutput, calls=%fused_computation.51 | convolution fusion | flops 1617952768 | bytes 10912768 | tf_op jit(solution)/shard_map/dot_general | solution.py:41
  293.2 8.7 %copy.87 = bf16[4096,768]{0,1:T(8,128)(2,1)} copy(bf16[4096,768]{1,0:T(8,128)(2,1)} %convolution_convert_fusion) | data formatting | bytes 12582912 | tf_op jit(solution)/shard_map/convert_element_type | solution.py:41
  301.9 17.9 %reshape.157 = bf16[64,64,3,8,32]{1,0,4,3,2:T(8,128)(2,1)} reshape(bf16[4096,768]{0,1:T(8,128)(2,1)} %copy.87) | data formatting | bytes 12582912 | tf_op jit(solution)/shard_map/reshape | solution.py:44
  319.7 8.3 %fusion.115 = (bf16[64,64,1,8,32]{1,0,4,3,2:T(8,128)(2,1)}, bf16[64,64,1,8,32]{1,0,4,3,2:T(8,128)(2,1)S(1)}, bf16[64,64,1,8,32]{1,0,4,3,2:T(8,128)(2,1)}) fusion(bf16[64,64,3,8,32]{1,0,4,3,2:T(8,128)(2,1)} %reshape.157), kind=kLoop, calls=%fused_computation.141 | loop fusion | bytes 12582912 | tf_op jit(solution)/shard_map/slice | solution.py:47
  328.0 19.8 %fusion.33 = (f32[64,8,64]{2,1,0:T(8,128)S(1)}, f32[64,8,64,64]{2,3,1,0:T(8,128)}) fusion(f32[8,64,64]{1,2,0:T(8,128)S(1)} %copy.91, bf16[64,64,1,8,32]{1,0,4,3,2:T(8,128)(2,1)} %get-tuple-element.7, bf16[64,64,1,8,32]{1,0,4,3,2:T(8,128)(2,1)S(1)} %get-tuple-element.6), kind=kOutput, calls=%fused_computation.41 | convolution fusion | flops 140476416 | bytes 12845056 | tf_op jit(solution)/shard_map/nqhd,nkhd->nhqk/dot_general | solution.py:50
  347.9 18.8 %convert_bitcast_fusion.1 = bf16[64,64,8,32]{1,3,2,0:T(8,128)(2,1)} fusion(f32[64,8,64,64]{2,3,1,0:T(8,128)} %get-tuple-element.35, f32[64,8,64]{2,1,0:T(8,128)S(1)} %get-tuple-element.34, f32[8,64,64]{1,2,0:T(8,128)S(1)} %copy.91, bf16[64,64,1,8,32]{1,0,4,3,2:T(8,128)(2,1)} %get-tuple-element.5), kind=kOutput, calls=%fused_computation.96 | convolution fusion | flops 143654912 | bytes 12845056 | tf_op jit(solution)/shard_map/nhqk,nkhd->nqhd/dot_general | solution.py:56
  366.7 7.1 %copy.93 = bf16[64,64,8,32]{1,0,3,2:T(8,128)(2,1)} copy(bf16[64,64,8,32]{1,3,2,0:T(8,128)(2,1)} %convert_bitcast_fusion.1) | data formatting | bytes 4194304 | tf_op jit(solution)/shard_map/convert_element_type | solution.py:57
  385.7 10.0 %fusion.51 = bf16[4096,256]{1,0:T(8,128)(2,1)} fusion(bf16[1024,256]{1,0:T(8,128)(2,1)S(1)} %copy-done.18, bf16[4096,256]{1,0:T(8,128)(2,1)} %copy-done.6, bf16[256,1024]{1,0:T(8,128)(2,1)} %param.38, f32[256]{0:T(256)S(1)} %bitcast.154, f32[4096]{0:T(1024)S(1)} %add_rsqrt_fusion.2, f32[4096]{0:T(1024)S(1)} %broadcast_multiply_fusion.2), kind=kOutput, calls=%fused_computation.66 | convolution fusion | flops 4341104640 | bytes 5276672 | tf_op jit(solution)/shard_map/dot_general | solution.py:66
  400.2 52.1 %all_to_all.10 = bf16[32,64,1,2,256]{4,1,3,2,0:T(8,128)(2,1)S(1)} all-to-all(bf16[32,64,1,2,256]{4,1,3,2,0:T(8,128)(2,1)S(1)} %bitcast.138), channel_id=1, replica_groups=mesh['row'=8,'col'=4] {'row','col'}, dimensions={0} | all-to-all | bytes 4194304 | tf_op jit(solution)/shard_map/all_to_all | solution.py:180
  (91 shorter events, 87.3 us)
Async XLA Ops:
  0.0 2.2 copy-start
  2.2 16.9 %copy-start.9 = (f32[8,64,64]{2,1,0:T(8,128)S(1)}, f32[8,64,64]{2,1,0:T(8,128)}, u32[]{:S(2)}) copy-start(f32[8,64,64]{2,1,0:T(8,128)} %param.31) | copy-start | bytes 393220
  2.2 17.0 %copy-start.13 = (f32[3,3,1024]{2,1,0:T(4,128)S(1)}, f32[3,3,1024]{2,1,0:T(4,128)}, u32[]{:S(2)}) copy-start(f32[3,3,1024]{2,1,0:T(4,128)} %param.25) | copy-start | bytes 110596
  9.4 3.2 copy-start.2
  12.6 17.5 %copy-start.14 = (f32[2,256]{1,0:T(2,128)S(1)}, f32[2,256]{1,0:T(2,128)}, u32[]{:S(2)}) copy-start(f32[2,256]{1,0:T(2,128)} %param.28) | copy-start | bytes 6148
  12.6 6.6 %collective-permute-start = (bf16[1,64,1024]{2,1,0:T(8,128)(2,1)S(1)}, bf16[1,64,1024]{2,1,0:T(8,128)(2,1)S(1)}, u32[]{:S(2)}, u32[]{:S(2)}) collective-permute-start(bf16[1,64,1024]{2,1,0:T(8,128)(2,1)S(1)} %get-tuple-element.15), channel_id=1, source_target_pairs={{0,4},{4,8},{8,12},{12,16},{16,20},{20,24},{24,28},{1,5},{5,9},{9,... | collective-permute-start | bytes 393224 | tf_op jit(solution)/shard_map/ppermute | solution.py:19
  17.1 6.3 %collective-permute-start.1 = (bf16[1,64,1024]{2,1,0:T(8,128)(2,1)S(1)}, bf16[1,64,1024]{2,1,0:T(8,128)(2,1)S(1)}, u32[]{:S(2)}, u32[]{:S(2)}) collective-permute-start(bf16[1,64,1024]{2,1,0:T(8,128)(2,1)S(1)} %get-tuple-element.16), channel_id=1, source_target_pairs={{4,0},{8,4},{12,8},{16,12},{20,16},{24,20},{28,24},{5,1},{9,5},{13... | collective-permute-start | bytes 393224 | tf_op jit(solution)/shard_map/ppermute | solution.py:22
  19.2 17.3 %copy-start.3 = (bf16[4096,1024]{1,0:T(8,128)(2,1)S(1)}, bf16[4096,1024]{1,0:T(8,128)(2,1)}, u32[]{:S(2)}) copy-start(bf16[4096,1024]{1,0:T(8,128)(2,1)} %copy-done.2) | copy-start | bytes 25165828
  25.5 6.9 %collective-permute-start.2 = (bf16[66,1,1024]{2,1,0:T(2,128)(2,1)S(1)}, bf16[66,1,1024]{2,1,0:T(2,128)(2,1)S(1)}, u32[]{:S(2)}, u32[]{:S(2)}) collective-permute-start(bf16[66,1,1024]{2,1,0:T(2,128)(2,1)S(1)} %get-tuple-element.13), channel_id=1, source_target_pairs={{0,1},{1,2},{2,3},{4,5},{5,6},{6,7},{8,9},{9,10},{10,11},{12,13},{... | collective-permute-start | bytes 405512 | tf_op jit(solution)/shard_map/ppermute | solution.py:19
  28.7 7.8 %collective-permute-start.3 = (bf16[66,1,1024]{2,1,0:T(2,128)(2,1)S(1)}, bf16[66,1,1024]{2,1,0:T(2,128)(2,1)S(1)}, u32[]{:S(2)}, u32[]{:S(2)}) collective-permute-start(bf16[66,1,1024]{2,1,0:T(2,128)(2,1)S(1)} %get-tuple-element.14), channel_id=1, source_target_pairs={{1,0},{2,1},{3,2},{5,4},{6,5},{7,6},{9,8},{10,9},{11,10},{13,12},{... | collective-permute-start | bytes 405512 | tf_op jit(solution)/shard_map/ppermute | solution.py:22
  30.2 20.1 %copy-start.16 = (bf16[1024,256]{1,0:T(8,128)(2,1)S(1)}, bf16[1024,256]{1,0:T(8,128)(2,1)}, u32[]{:S(2)}) copy-start(bf16[1024,256]{1,0:T(8,128)(2,1)} %param.27) | copy-start | bytes 1572868
  30.2 20.1 %copy-start.19 = (f32[1024]{0:T(1024)S(1)}, f32[1024]{0:T(1024)}, u32[]{:S(2)}) copy-start(f32[1024]{0:T(1024)} %param.26) | copy-start | bytes 12292
  82.9 6.5 %copy-start.4 = (bf16[64,64,256]{2,1,0:T(8,128)(2,1)S(1)}, bf16[64,64,256]{2,1,0:T(8,128)(2,1)}, u32[]{:S(2)}) copy-start(bf16[64,64,256]{2,1,0:T(8,128)(2,1)} %fusion.70) | copy-start | bytes 6291460
  90.8 8.1 %copy-start.7 = (bf16[256,768]{1,0:T(8,128)(2,1)S(1)}, bf16[256,768]{1,0:T(8,128)(2,1)}, u32[]{:S(2)}) copy-start(bf16[256,768]{1,0:T(8,128)(2,1)} %param.29) | copy-start | bytes 1179652
  178.2 12.8 %copy-start.11 = (bf16[256,256]{1,0:T(8,128)(2,1)S(1)}, bf16[256,256]{1,0:T(8,128)(2,1)}, u32[]{:S(2)}) copy-start(bf16[256,256]{1,0:T(8,128)(2,1)} %param.30) | copy-start | bytes 393220
  185.3 11.9 %copy-start.17 = (bf16[1024,256]{1,0:T(8,128)(2,1)S(1)}, bf16[1024,256]{1,0:T(8,128)(2,1)}, u32[]{:S(2)}) copy-start(bf16[1024,256]{1,0:T(8,128)(2,1)} %param.33) | copy-start | bytes 1572868
  194.6 1.3 copy-start.5
  206.2 8.9 %copy-start.10 = (f32[8,64,64]{2,1,0:T(8,128)S(1)}, f32[8,64,64]{2,1,0:T(8,128)}, u32[]{:S(2)}) copy-start(f32[8,64,64]{2,1,0:T(8,128)} %param.37) | copy-start | bytes 393220
  206.2 9.1 %copy-start.15 = (f32[2,256]{1,0:T(2,128)S(1)}, f32[2,256]{1,0:T(2,128)}, u32[]{:S(2)}) copy-start(f32[2,256]{1,0:T(2,128)} %param.34) | copy-start | bytes 6148
  208.2 55.1 %all-to-all-start = ((bf16[32,64,1,2,256]{4,1,3,2,0:T(8,128)(2,1)}), bf16[32,64,1,2,256]{4,1,3,2,0:T(8,128)(2,1)S(1)}, u32[]{:S(2)}, u32[]{:S(2)}) async-start(bf16[32,64,1,2,256]{4,1,3,2,0:T(8,128)(2,1)} %copy.85), calls=%async_computation | async-start | bytes 4194304 | tf_op jit(solution)/shard_map/all_to_all | solution.py:150
  272.4 14.4 %copy-start.8 = (bf16[256,768]{1,0:T(8,128)(2,1)S(1)}, bf16[256,768]{1,0:T(8,128)(2,1)}, u32[]{:S(2)}) copy-start(bf16[256,768]{1,0:T(8,128)(2,1)} %param.35) | copy-start | bytes 1179652
  366.7 12.8 %copy-start.12 = (bf16[256,256]{1,0:T(8,128)(2,1)S(1)}, bf16[256,256]{1,0:T(8,128)(2,1)}, u32[]{:S(2)}) copy-start(bf16[256,256]{1,0:T(8,128)(2,1)} %param.36) | copy-start | bytes 393220
  373.8 11.9 %copy-start.18 = (bf16[1024,256]{1,0:T(8,128)(2,1)S(1)}, bf16[1024,256]{1,0:T(8,128)(2,1)}, u32[]{:S(2)}) copy-start(bf16[1024,256]{1,0:T(8,128)(2,1)} %param.39) | copy-start | bytes 1572868
  398.5 55.5 %copy-start.1 = (bf16[256,1024]{1,0:T(8,128)(2,1)S(1)}, bf16[256,1024]{1,0:T(8,128)(2,1)}, u32[]{:S(2)}) copy-start(bf16[256,1024]{1,0:T(8,128)(2,1)} %param.23) | copy-start | bytes 1572868
  (1 other events, 1.3 us)
where the time goes:
time: 459 us; the launch traced here: 454 us
  matrix products  155 us (34%)
  local copies, waits for them, and re-layouts  127 us (28%)
  waiting for transfers between devices  58.4 us (13%)
  blocking collectives  52.1 us (11%)
  other arithmetic  42.9 us (9%)
  starting transfers between devices  18.1 us (4%)
    all_to_all x1, blocking collectives, shards(): lax.all_to_all(returning, ('row', 'col'), split_axis=0, concat_axis=0, ti...  52.1 us
    all_to_all x1, waiting for transfers between devices, shards(): lax.all_to_all(outgoing, ('row', 'col'), split_axis=0, concat_axis=0, til...  48 us
    dot_general x2, matrix products, attend(): jnp.einsum('nqhd,nkhd->nhqk', query_rows, key_rows, preferred_element_typ...  40.1 us
    dot_general x2, matrix products, attend(): jnp.einsum('nhqk,nkhd->nqhd', weights, value_rows, preferred_element_type...  38.3 us
    reshape x2, local copies, waits for them, and re-layouts, attend(): projected.reshape(win_count, positions, 3, head_count, head_size)  35.7 us
    dot_general x1, matrix products, shards(): jnp.dot(activated.reshape(-1, inner_width), project_weight, preferred_ele...  32.6 us
    dot_general x2, matrix products, attend(): jnp.dot(hidden, shrink_weight, preferred_element_type=jnp.float32)  18.9 us
    convert_element_type x2, local copies, waits for them, and re-layouts, attend(): jnp.dot(lifted, entry_weight, preferred_element_type=jnp.float32)  17.4 us
  transfers between devices with their start and end apart: 5, of which 4 were waited for; matrix products, arithmetic and copies ran while one was open for 0% of the time, Pallas kernels for 0%

commit v1 on v0

v1 whole, which is shorter than its diff:
```python
import functools
import math

import jax
import jax.numpy as jnp
from jax import lax
from jax.experimental import pallas as pl
from jax.experimental.pallas import tpu as pltpu
from jax.sharding import PartitionSpec as P

WIN = 8
LAG = 2
LANES = 128
MESH = pl.DeviceIdType.MESH

epsilon = 1e-05
f32 = jnp.float32
bf16 = jnp.bfloat16


def gelu(v):
    c = math.sqrt(2.0 / math.pi)
    return v * (0.5 + 0.5 * jnp.tanh(v * (c + (c * 0.044715) * (v * v))))


def dot(a, b):
    return jnp.dot(a, b, preferred_element_type=f32)


def dot_t(a, b):
    return lax.dot_general(a, b, (((1,), (1,)), ((), ())), preferred_element_type=f32)


def layer_norm(values, gain_row):
    center = values - jnp.mean(values, axis=-1, keepdims=True)
    spread = jnp.mean(center * center, axis=-1, keepdims=True)
    return (center * lax.rsqrt(spread + epsilon) * gain_row).astype(bf16)


def attend(x, heads, gains, entry, leave, offsets, widen, shrink, mask, ones, exps, mixed):
    tokens, channels = x.shape
    positions = WIN * WIN
    windows = tokens // positions
    scale = 1.0 / math.sqrt(channels // heads)
    projected = dot(layer_norm(x, gains[0:1]), entry[...]).astype(bf16)
    for w in range(windows):
        span = slice(w * positions, (w + 1) * positions)
        key = projected[span, channels : 2 * channels]
        spread = jnp.concatenate([key] * heads, axis=0) * mask[...]
        scores = dot_t(projected[span, :channels], spread) * scale + offsets[...]
        exps[span, :] = jnp.exp(scores).astype(bf16)
    for w in range(windows):
        span = slice(w * positions, (w + 1) * positions)
        value = projected[span, 2 * channels :]
        spread = jnp.concatenate([value] * heads, axis=0) * mask[...]
        e = exps[span, :]
        total = dot(e, ones[...])
        weights = (e.astype(f32) / total).astype(bf16)
        mixed[span, :] = dot(weights, spread).astype(bf16)
    attended = (x + dot(mixed[...], leave[...])).astype(bf16).astype(f32)
    second = layer_norm(attended, gains[1:2])
    result = attended
    width = widen.shape[1]
    for part in range(0, width, 256):
        hidden = gelu(dot(second, widen[:, part : part + 256])).astype(bf16)
        result = result + dot(hidden, shrink[part : part + 256, :])
    return result


def kernel(
    dims, xpad, side, cscale, cshift, ew, eb, dk, db, pw,
    bg, be, bl, bo, bw, bs, gg, ge, gl, go, gw, gs, mask, ones, perm, unperm,
    out, ex, side_ex, side_sum, act, exps, mixed, snd, rcv, bsnd,
    send_sem, recv_sem, bsend_sem, brecv_sem,
):
    heads, rp, cp, rg, cg, hc = dims
    group = rg * cg
    rows_here = xpad.shape[0] - 2
    cols_here, channels = xpad.shape[1:]
    inner = ew.shape[1]
    strips = rows_here // WIN
    r, c = lax.axis_index("row"), lax.axis_index("col")
    n_row, n_col = lax.axis_size("row"), lax.axis_size("col")
    me = (r // rp) * cg + c // cp

    def device(slot):
        return ((slot // cg) * rp + lax.rem(r, rp), lax.rem(slot, cg) * cp + lax.rem(c, cp))

    barrier = pltpu.get_barrier_semaphore()

    def greet(d, carry):
        pl.semaphore_signal(
            barrier, inc=1, device_id=device(lax.rem(me + d, group)), device_id_type=MESH
        )
        return carry

    lax.fori_loop(1, group, greet, 0)

    top = (r > 0).astype(f32)
    bottom = (r < n_row - 1).astype(f32)
    left = (c > 0).astype(f32)
    right = (c < n_col - 1).astype(f32)

    def expand(cells, part):
        normed = (cells.astype(f32) * cscale[...] + cshift[...]).astype(bf16)
        lanes = slice(part, part + 256)
        return gelu(dot(normed, ew[:, lanes]) + eb[:, lanes])

    for which in range(2):
        depth = side.shape[1]
        at = lax.broadcasted_iota(jnp.int32, (depth, 256), 0)
        keep = jnp.where(at == 0, top, jnp.where(at == rows_here + 1, bottom, 1.0))
        keep = keep * (left if which == 0 else right)
        for part in range(0, inner, 256):
            side_ex[:, part : part + 256] = expand(side[which], part) * keep
        tap = 0 if which == 0 else 2
        total = side_ex[0:rows_here, :] * dk[tap : tap + 1, :]
        for s in range(1, 3):
            total = total + side_ex[s : s + rows_here, :] * dk[3 * s + tap : 3 * s + tap + 1, :]
        side_sum[which] = total
    for part in range(0, inner, 256):
        first = expand(xpad[0:2].reshape(2 * cols_here, channels), part)
        ex[0:2, :, part : part + 256] = first.reshape(2, cols_here, 256)
    ex[0] = ex[0] * top

    pl.semaphore_wait(barrier, group - 1)

    def send_all(source, target, index, sem_out, sem_in):
        def one(d, carry):
            slot = lax.rem(me + d, group)
            pltpu.make_async_remote_copy(
                src_ref=source.at[index, slot],
                dst_ref=target.at[index, me],
                send_sem=sem_out.at[index],
                recv_sem=sem_in.at[index],
                device_id=device(slot),
                device_id_type=MESH,
            ).start()
            return carry

        lax.fori_loop(1, group, one, 0)

    def await_bytes(ref, index, count, sem):
        part = ref.at[index, pl.ds(0, count)]
        pltpu.make_async_copy(part, part, sem.at[index]).wait()

    def block_strip(i):
        base = i * WIN
        cells = xpad[pl.ds(base + 2, WIN)].reshape(WIN * cols_here, channels)
        for part in range(0, inner, 256):
            grown = expand(cells, part).reshape(WIN, cols_here, 256)
            ex[pl.ds(base + 2, WIN), :, part : part + 256] = grown

        @pl.when(i == strips - 1)
        def _():
            ex[rows_here + 1] = ex[rows_here + 1] * bottom

        near = pl.ds(pl.multiple_of(base, WIN), WIN)

        def chunk(j, carry):
            lanes = pl.ds(pl.multiple_of(j * LANES, LANES), LANES)
            col = lax.broadcasted_iota(jnp.int32, (cols_here, LANES), 0)
            taps = [dk[n : n + 1, lanes] for n in range(9)]
            bias = db[:, lanes]
            lsum = side_sum[0, near, lanes]
            rsum = side_sum[1, near, lanes]
            rows = [ex[base + n, :, lanes] for n in range(WIN + 2)]
            for y in range(WIN):
                a = [
                    taps[t] * rows[y] + taps[3 + t] * rows[y + 1] + taps[6 + t] * rows[y + 2]
                    for t in range(3)
                ]
                low = jnp.where(col == 0, lsum[y : y + 1], pltpu.roll(a[0], 1, 0))
                high = jnp.where(
                    col == cols_here - 1, rsum[y : y + 1], pltpu.roll(a[2], cols_here - 1, 0)
                )
                act[y * cols_here : (y + 1) * cols_here, lanes] = gelu(
                    low + a[1] + high + bias
                ).astype(bf16)
            return carry

        lax.fori_loop(0, inner // LANES, chunk, 0)
        source = xpad[pl.ds(base + 1, WIN)].reshape(WIN * cols_here, channels)
        one = source.astype(f32) + dot(act[...], pw[...])
        one = one.reshape(WIN, cols_here // WIN, WIN, channels).transpose(1, 0, 2, 3)
        one = one.reshape(-1, channels).astype(bf16).astype(f32)
        two = attend(one, heads, bg, be, bl, bo, bw, bs, mask, ones, exps, mixed)
        two = two.reshape(hc, cg, rg, WIN, channels).transpose(2, 1, 0, 3, 4)
        snd[i] = two.reshape(group, hc * WIN, channels).astype(bf16)
        send_all(snd, rcv, i, send_sem, recv_sem)
        rcv[i, me] = snd[i, me]

    def grid_strip(i):
        await_bytes(rcv, i, group - 1, recv_sem)
        tokens = rcv[i].reshape(group * hc * WIN, channels)
        tokens = dot(perm[...], tokens)
        done = attend(tokens, heads, gg, ge, gl, go, gw, gs, mask, ones, exps, mixed)
        done = dot(unperm[...], done.astype(bf16))
        bsnd[i] = done.reshape(group, hc * WIN, channels).astype(bf16)
        send_all(bsnd, out, i, bsend_sem, brecv_sem)
        pltpu.make_async_copy(bsnd.at[i, me], out.at[i, me], brecv_sem.at[i]).start()

    def step(i, carry):
        @pl.when(i < strips)
        def _():
            block_strip(i)

        @pl.when(i >= LAG)
        def _():
            grid_strip(i - LAG)

        return carry

    lax.fori_loop(0, strips + LAG, step, 0)

    def finish(i, carry):
        await_bytes(snd, i, group - 1, send_sem)
        await_bytes(bsnd, i, group - 1, bsend_sem)
        await_bytes(out, i, group, brecv_sem)
        return carry

    lax.fori_loop(0, strips, finish, 0)


def halo(tile):
    def shifted(piece, axis, up):
        count = lax.axis_size(axis)
        pairs = [(i, i + 1) if up else (i + 1, i) for i in range(count - 1)]
        return lax.ppermute(piece, axis, pairs)

    above = shifted(tile[-1:], "row", True)
    below = shifted(tile[:1], "row", False)
    first = jnp.concatenate([above[:, 0], tile[:, 0], below[:, 0]], axis=0)
    last = jnp.concatenate([above[:, -1], tile[:, -1], below[:, -1]], axis=0)
    before = shifted(last, "col", True)
    after = shifted(first, "col", False)
    return jnp.concatenate([above, tile, below], axis=0), jnp.stack([before, after])


def shards(
    radar_tiles, conv_scale, conv_shift, expand_weight, expand_bias, depth_kernel, depth_bias,
    project_weight, block_gains, block_entry, block_leave, block_offsets, block_widen,
    block_shrink, grid_gains, grid_entry, grid_leave, grid_offsets, grid_widen, grid_shrink,
):
    rows_here, cols_here, channels = radar_tiles.shape
    inner = expand_weight.shape[1]
    heads = block_offsets.shape[0]
    n_row, n_col = lax.axis_size("row"), lax.axis_size("col")
    rp, cp = max(1, n_row // WIN), max(1, n_col // WIN)
    rg, cg = min(n_row, WIN), min(n_col, WIN)
    hc = WIN // cg
    group = rg * cg
    strips = rows_here // WIN
    positions = WIN * WIN
    tokens = WIN * cols_here
    xpad, side = halo(radar_tiles)
    side = jnp.pad(side, ((0, 0), (0, -side.shape[1] % 16), (0, 0)))

    def laid(offsets):
        return offsets.transpose(1, 0, 2).reshape(positions, heads * positions)

    at = jnp.arange(heads * positions)
    mask = (at[:, None] // positions == jnp.arange(channels)[None] // (channels // heads)).astype(bf16)
    ones = (at[:, None] // positions == at[None] // positions).astype(bf16)
    order = jnp.arange(tokens)
    source = (order % positions) * WIN + order // positions
    perm = (source[:, None] == order[None]).astype(bf16)
    unperm = (source[None] == order[:, None]).astype(bf16)
    chunk = (strips, group, hc * WIN, channels)
    vmem = pl.BlockSpec(memory_space=pltpu.VMEM)
    operands = (
        xpad, side, conv_scale[None], conv_shift[None], expand_weight, expand_bias[None],
        depth_kernel.reshape(9, inner), depth_bias[None], project_weight,
        block_gains, block_entry, block_leave, laid(block_offsets), block_widen, block_shrink,
        grid_gains, grid_entry, grid_leave, laid(grid_offsets), grid_widen, grid_shrink,
        mask, ones, perm, unperm,
    )
    returned = pl.pallas_call(
        functools.partial(kernel, (heads, rp, cp, rg, cg, hc)),
        out_shape=jax.ShapeDtypeStruct(chunk, bf16),
        in_specs=[vmem] * len(operands),
        out_specs=pl.BlockSpec(memory_space=pl.ANY),
        scratch_shapes=[
            pltpu.VMEM((rows_here + 2, cols_here, inner), f32),
            pltpu.VMEM((side.shape[1], inner), f32),
            pltpu.VMEM((2, rows_here, inner), f32),
            pltpu.VMEM((tokens, inner), bf16),
            pltpu.VMEM((tokens, heads * positions), bf16),
            pltpu.VMEM((tokens, channels), bf16),
            pltpu.VMEM(chunk, bf16),
            pltpu.VMEM(chunk, bf16),
            pltpu.VMEM(chunk, bf16),
            pltpu.SemaphoreType.DMA((strips,)),
            pltpu.SemaphoreType.DMA((strips,)),
            pltpu.SemaphoreType.DMA((strips,)),
            pltpu.SemaphoreType.DMA((strips,)),
        ],
        compiler_params=pltpu.CompilerParams(
            collective_id=0, has_side_effects=True, vmem_limit_bytes=58 * 2**20
        ),
    )(*operands)
    returned = returned.reshape(strips, rg, cg, hc, WIN, channels).transpose(0, 1, 3, 2, 4, 5)
    return returned.reshape(rows_here, cols_here, channels)


def solution(mesh):
    return jax.shard_map(
        shards,
        mesh=mesh,
        in_specs=(P("row", "col", None),) + (P(),) * 19,
        out_specs=P("row", "col", None),
        check_vma=False,
    )
```

time: 459 us -> 154 us (0.34)
  matrix products: 155 us -> 0 us
  Pallas kernels: 0 us -> 129 us
  local copies, waits for them, and re-layouts: 127 us -> 7.85 us
  waiting for transfers between devices: 58.4 us -> 0.01 us
  blocking collectives: 52.1 us -> 0 us
  other arithmetic: 42.9 us -> 4.53 us
  starting transfers between devices: 18.1 us -> 11.7 us
    dot_general x12 -> x0, matrix products: 155 us -> none  [the longest x2 40.1 us: attend(): jnp.einsum('nqhd,nkhd->nhqk', query_rows, key_rows, preferred_element_typ...]
    pallas_call x0 -> x1, Pallas kernels: none -> 129 us  [shards(): pl.pallas_call(functools.partial(kernel, (heads, rp, cp, rg, cg, hc)), ou...]
    all_to_all x1 -> x0, blocking collectives: 52.1 us -> none  [shards(): lax.all_to_all(returning, ('row', 'col'), split_axis=0, concat_axis=0, ti...]
    all_to_all x1 -> x0, waiting for transfers between devices: 48 us -> none  [shards(): lax.all_to_all(outgoing, ('row', 'col'), split_axis=0, concat_axis=0, til...]
    convert_element_type x7 -> x0, local copies, waits for them, and re-layouts: 46.6 us -> none  [the longest x2 17.4 us: attend(): jnp.dot(lifted, entry_weight, preferred_element_type=jnp.float32)]
    reshape x5 -> x3, local copies, waits for them, and re-layouts: 48.6 us -> 2.19 us  [the longest x2 1.55 us: laid(): return offsets.transpose(1, 0, 2).reshape(positions, heads * positions)]
    reduce_sum x6 -> x0, other arithmetic: 16.7 us -> none  [the longest x4 10.1 us: layer_norm(): spread = jnp.mean(center * center, axis=-1, keepdims=True)]
    slice x6 -> x2, local copies, waits for them, and re-layouts: 16.8 us -> 2.13 us  [the longest x1 1.29 us: halo(): last = jnp.concatenate([above[:, -1], tile[:, -1], below[:, -1]], axis=0)]
  transfers between devices with their start and end apart: 5 -> 4, of which waited for: 4 -> 0; matrix products, arithmetic and copies ran while one was open for 0% -> 5% of each run, Pallas kernels for 0% -> 0%
where the time goes in v1:
time: 154 us
  Pallas kernels  129 us (84%)
  starting transfers between devices  11.7 us (8%)
  local copies, waits for them, and re-layouts  7.85 us (5%)
  other arithmetic  4.53 us (3%)
    pallas_call x1, Pallas kernels, shards(): pl.pallas_call(functools.partial(kernel, (heads, rp, cp, rg, cg, hc)), ou...  129 us
    ppermute x4, starting transfers between devices, shifted(): return lax.ppermute(piece, axis, pairs)  11.7 us
    transpose x1, local copies, waits for them, and re-layouts, shards(): returned.reshape(strips, rg, cg, hc, WIN, channels)  3.18 us
  transfers between devices with their start and end apart: 4, of which 0 were waited for; matrix products, arithmetic and copies ran while one was open for 5% of the time, Pallas kernels for 0%

profile of v1, /device:TPU:1, one launch (start us, length us, event | category | flops | bytes accessed | tf_op | source)
XLA Modules:
  0.0 153.5 jit_solution(7814726691597427967)
XLA Ops:
  0.0 0.8 fusion.15
  0.9 4.5 %collective-permute-start = (bf16[1,64,256]{2,1,0:T(8,128)(2,1)S(1)}, bf16[1,64,256]{2,1,0:T(8,128)(2,1)S(1)}, u32[]{:S(2)}, u32[]{:S(2)}) collective-permute-start(bf16[1,64,256]{2,1,0:T(8,128)(2,1)S(1)} %get-tuple-element.7), channel_id=1, source_target_pairs={{0,4},{4,8},{8,12},{12,16},{16,20},{20,24},{24,28},{1,5},{5,9},{9,... | collective-permute-start | bytes 98312 | tf_op jit(solution)/shard_map/ppermute | solution.py:229
  5.4 1.9 %collective-permute-start.1 = (bf16[1,64,256]{2,1,0:T(8,128)(2,1)S(1)}, bf16[1,64,256]{2,1,0:T(8,128)(2,1)S(1)}, u32[]{:S(2)}, u32[]{:S(2)}) collective-permute-start(bf16[1,64,256]{2,1,0:T(8,128)(2,1)S(1)} %get-tuple-element.8), channel_id=1, source_target_pairs={{4,0},{8,4},{12,8},{16,12},{20,16},{24,20},{28,24},{5,1},{9,5},{13... | collective-permute-start | bytes 98312 | tf_op jit(solution)/shard_map/ppermute | solution.py:229
  7.3 0.0 copy-start
  7.3 1.3 fusion.14
  8.6 1.4 fusion.1
  10.0 0.9 compare_convert_fusion.1.mask
  10.8 0.0 copy-done.3
  10.8 0.6 reshape.150.dk
  11.5 0.0 copy-done.1
  11.5 0.2 copy.23
  11.7 0.8 reshape.151.bo
  12.4 0.2 copy.24
  12.6 0.8 reshape.152.go
  13.4 0.0 collective-permute-done
  13.4 0.0 collective-permute-done.1
  13.4 1.3 collective-permute-start.3
  14.8 4.0 %collective-permute-start.2 = (bf16[66,256]{1,0:T(8,128)(2,1)S(1)}, bf16[66,256]{1,0:T(8,128)(2,1)S(1)}, u32[]{:S(2)}, u32[]{:S(2)}) collective-permute-start(bf16[66,256]{1,0:T(8,128)(2,1)S(1)} %pad_maximum_fusion.1), channel_id=1, source_target_pairs={{0,1},{1,2},{2,3},{4,5},{5,6},{6,7},{8,9},{9,10},{10,11},{12,13},{... | collective-permute-start | bytes 101384 | tf_op jit(solution)/shard_map/ppermute | solution.py:229
  18.8 1.6 %pad_maximum_fusion.xpad = bf16[66,64,256]{2,1,0:T(8,128)(2,1)} fusion(bf16[1,64,256]{2,1,0:T(8,128)(2,1)S(1)} %collective-permute-done.1, bf16[64,64,256]{2,1,0:T(8,128)(2,1)S(1)} %copy-done, bf16[1,64,256]{2,1,0:T(8,128)(2,1)S(1)} %collective-permute-done), kind=kLoop, calls=%fused_computation | loop fusion | flops 2162688 | bytes 4325376 | tf_op jit(solution)/shard_map/concatenate | solution.py:237
  20.4 0.0 collective-permute-done.3
  20.4 0.0 collective-permute-done.2
  20.4 0.6 fusion.4.side
  21.0 129.3 %shard_map.190 = bf16[8,32,16,256]{3,2,1,0:T(8,128)(2,1)} custom-call(bf16[66,64,256]{2,1,0:T(8,128)(2,1)} %pad_maximum_fusion.xpad, bf16[2,80,256]{2,1,0:T(8,128)(2,1)} %fusion.4.side, f32[1,256]{1,0:T(1,128)} %bitcast.35, f32[1,256]{1,0:T(1,128)} %bitcast.36, bf16[256,1024]{1,0:T(8,128)(2,1)} %ew.1, f32[1,1024]{1,0:T(1,128)} %bitcast.33, ...), custom_call_target="tpu_custom_call" | custom-call | tf_op jit(solution)/shard_map/pallas_call | solution.py:278
  150.3 3.2 %copy.25 = bf16[8,8,2,4,8,256]{5,4,3,2,1,0:T(8,128)(2,1)} copy(bf16[8,8,2,4,8,256]{5,4,2,3,1,0:T(8,128)(2,1)} %bitcast.26) | data formatting | bytes 4194304 | tf_op jit(solution)/shard_map/transpose | solution.py:302
  (14 shorter events, 0.1 us)
Async XLA Ops:
  0.0 10.8 %copy-start.3 = (f32[3,3,1024]{2,1,0:T(4,128)S(1)}, f32[3,3,1024]{2,1,0:T(4,128)}, u32[]{:S(2)}) copy-start(f32[3,3,1024]{2,1,0:T(4,128)} %param.25) | copy-start | bytes 110596
  0.0 11.5 %copy-start.1 = (f32[8,64,64]{2,1,0:T(8,128)S(1)}, f32[8,64,64]{2,1,0:T(8,128)}, u32[]{:S(2)}) copy-start(f32[8,64,64]{2,1,0:T(8,128)} %param.31) | copy-start | bytes 393220
  0.0 12.4 %copy-start.2 = (f32[8,64,64]{2,1,0:T(8,128)S(1)}, f32[8,64,64]{2,1,0:T(8,128)}, u32[]{:S(2)}) copy-start(f32[8,64,64]{2,1,0:T(8,128)} %param.37) | copy-start | bytes 393220
  0.9 12.5 %collective-permute-start = (bf16[1,64,256]{2,1,0:T(8,128)(2,1)S(1)}, bf16[1,64,256]{2,1,0:T(8,128)(2,1)S(1)}, u32[]{:S(2)}, u32[]{:S(2)}) collective-permute-start(bf16[1,64,256]{2,1,0:T(8,128)(2,1)S(1)} %get-tuple-element.7), channel_id=1, source_target_pairs={{0,4},{4,8},{8,12},{12,16},{16,20},{20,24},{24,28},{1,5},{5,9},{9,... | collective-permute-start | bytes 98312 | tf_op jit(solution)/shard_map/ppermute | solution.py:229
  5.4 8.0 %collective-permute-start.1 = (bf16[1,64,256]{2,1,0:T(8,128)(2,1)S(1)}, bf16[1,64,256]{2,1,0:T(8,128)(2,1)S(1)}, u32[]{:S(2)}, u32[]{:S(2)}) collective-permute-start(bf16[1,64,256]{2,1,0:T(8,128)(2,1)S(1)} %get-tuple-element.8), channel_id=1, source_target_pairs={{4,0},{8,4},{12,8},{16,12},{20,16},{24,20},{28,24},{5,1},{9,5},{13... | collective-permute-start | bytes 98312 | tf_op jit(solution)/shard_map/ppermute | solution.py:229
  7.3 11.4 %copy-start = (bf16[64,64,256]{2,1,0:T(8,128)(2,1)S(1)}, bf16[64,64,256]{2,1,0:T(8,128)(2,1)}, u32[]{:S(2)}) copy-start(bf16[64,64,256]{2,1,0:T(8,128)(2,1)} %param.20) | copy-start | bytes 6291460
  13.4 7.0 %collective-permute-start.3 = (bf16[66,256]{1,0:T(8,128)(2,1)S(1)}, bf16[66,256]{1,0:T(8,128)(2,1)S(1)}, u32[]{:S(2)}, u32[]{:S(2)}) collective-permute-start(bf16[66,256]{1,0:T(8,128)(2,1)S(1)} %pad_maximum_fusion.2), channel_id=1, source_target_pairs={{1,0},{2,1},{3,2},{5,4},{6,5},{7,6},{9,8},{10,9},{11,10},{13,12},{... | collective-permute-start | bytes 101384 | tf_op jit(solution)/shard_map/ppermute | solution.py:229
  14.8 5.6 %collective-permute-start.2 = (bf16[66,256]{1,0:T(8,128)(2,1)S(1)}, bf16[66,256]{1,0:T(8,128)(2,1)S(1)}, u32[]{:S(2)}, u32[]{:S(2)}) collective-permute-start(bf16[66,256]{1,0:T(8,128)(2,1)S(1)} %pad_maximum_fusion.1), channel_id=1, source_target_pairs={{0,1},{1,2},{2,3},{4,5},{5,6},{6,7},{8,9},{9,10},{10,11},{12,13},{... | collective-permute-start | bytes 101384 | tf_op jit(solution)/shard_map/ppermute | solution.py:229
